TPU v7x, 32 devices: a whole 2x2x4 slice. The times are simulated.
32 devices in a mesh: batch: 8 (over y, x, core), mp: 4 (over z).
Axes of the slice: x: 2, y: 2, z: 4, core: 2. Of those that a mesh axis runs over, the one named last changes fastest.
Arguments:
- residual: bfloat16 [8, 64, 8192], P('batch', None, 'mp'), may hold values from -6 to 6
- query_states: bfloat16 [8, 64, 4096], P('batch', None, 'mp')
- key_states: bfloat16 [8, 64, 512], P('batch')
- value_states: bfloat16 [8, 64, 512], P('batch'), may hold values from -6 to 6
- prompt_perm: int32 [8], replicated, may hold values from 0 to 7, each once
- ablated_heads: int32 [8], replicated, may hold values from 0 to 31, as said below
- out_weight: bfloat16 [4096, 8192], P('batch', 'mp'), may hold values from -0.09375 to 0.09375
- rms_gain: float32 [8192], P('mp'), may hold values from 0.1 to 1.9
- gate_weight: bfloat16 [8192, 14336], P('mp', 'batch'), may hold values from -0.0625 to 0.0625
- up_weight: bfloat16 [8192, 14336], P('mp', 'batch'), may hold values from -0.0625 to 0.0625
- down_weight: bfloat16 [14336, 8192], P('batch', 'mp'), may hold values from -0.046875 to 0.046875
Outputs:
- attn_out: bfloat16 [8, 64, 8192], P('batch', None, 'mp')
- mlp_out: bfloat16 [8, 64, 8192], P('batch', None, 'mp')
Inputs may be any that keep to these rules, and one draw needn't show every extreme that they name: `prompt_perm`: each prompt index appears exactly once. `ablated_heads`: 8 different head indices in any order, one of them 32 - 1.
All inputs are finite; a program needn't handle non-finite values.
Results may differ from a plain program's by a relative error of at most 0.035.
Values may be sent and summed in bfloat16 or wider, within the bound.
A program may use at most 128 MiB of HBM per device.

v0:
```python
import math
import jax
import jax.numpy as jnp
from jax import lax
from jax.sharding import PartitionSpec as P

D = 8192
HEADS = 32
KV = 4
HD = 128
ABLATED = 8


def local_heads(query_states, key_states, value_states):
    prompts_here, length, columns = query_states.shape
    head_count = columns // HD
    first_head = lax.axis_index("mp") * head_count
    owners = (first_head + jnp.arange(head_count)) // (HEADS // KV)
    query_four = query_states.reshape(prompts_here, length, head_count, HD)
    key_four = jnp.take(key_states.reshape(prompts_here, length, KV, HD), owners, axis=2)
    value_four = jnp.take(value_states.reshape(prompts_here, length, KV, HD), owners, axis=2)
    scores = jnp.einsum(
        "pshd,pthd->phst", query_four, key_four, preferred_element_type=jnp.float32
    ) / math.sqrt(HD)
    positions = jnp.arange(length)
    causal = positions[:, None] >= positions[None, :]
    scores = jnp.where(causal, scores, -1e30)
    highest = jnp.max(scores, axis=-1, keepdims=True)
    weights = jnp.exp(scores - highest)
    probability = (weights / jnp.sum(weights, axis=-1, keepdims=True)).astype(jnp.bfloat16)
    mixed_heads = jnp.einsum(
        "phst,pthd->pshd", probability, value_four, preferred_element_type=jnp.float32
    )
    return mixed_heads.astype(jnp.bfloat16).reshape(prompts_here, length, head_count * HD)


def body(
    residual,
    query_states,
    key_states,
    value_states,
    prompt_perm,
    ablated_heads,
    out_weight,
    rms_gain,
    gate_weight,
    up_weight,
    down_weight,
):
    prompts_here, length, model_cols = residual.shape
    local_rows = prompts_here * length
    head_block = local_heads(query_states, key_states, value_states)
    all_heads = lax.all_gather(head_block, "mp", axis=2, tiled=True)
    batch_index = lax.axis_index("batch")
    sources = jnp.take(prompt_perm, batch_index * prompts_here + jnp.arange(prompts_here))
    stacked = all_heads.reshape(prompts_here, length, HEADS, HD)
    picked_cols = jnp.take(stacked, ablated_heads, axis=2).reshape(
        prompts_here, length * ABLATED * HD
    )
    block_rows = lax.all_gather(picked_cols, "batch", axis=0, tiled=True)
    selector = (sources[:, None] == jnp.arange(block_rows.shape[0])[None, :]).astype(jnp.bfloat16)
    picked = jnp.dot(selector, block_rows, preferred_element_type=jnp.float32)
    picked_four = picked.astype(jnp.bfloat16).reshape(prompts_here, length, ABLATED, HD)
    placing = (jnp.arange(HEADS)[:, None] == ablated_heads[None, :]).astype(jnp.bfloat16)
    placed = jnp.einsum(
        "psad,ga->psgd", picked_four, placing, preferred_element_type=jnp.float32
    ).astype(jnp.bfloat16)
    chosen = jnp.any(jnp.arange(HEADS)[:, None] == ablated_heads[None, :], axis=1)
    mixed_heads = jnp.where(chosen[None, None, :, None], placed, stacked).reshape(
        local_rows, HEADS * HD
    )
    attn_float = jnp.dot(
        mixed_heads,
        lax.all_gather(out_weight, "batch", axis=0, tiled=True),
        preferred_element_type=jnp.float32,
    )
    attn_out = attn_float.astype(jnp.bfloat16)
    hidden_state = residual.reshape(local_rows, model_cols).astype(jnp.float32) + attn_float
    squares = lax.psum(jnp.sum(hidden_state * hidden_state, axis=1), "mp")
    inverse = lax.rsqrt(squares / D + 1e-05)
    normed = (hidden_state * inverse[:, None] * rms_gain[None, :]).astype(jnp.bfloat16)
    block_rows = lax.all_gather(normed, "batch", axis=0, tiled=True)
    gate_part = jnp.dot(block_rows, gate_weight, preferred_element_type=jnp.float32)
    up_part = jnp.dot(block_rows, up_weight, preferred_element_type=jnp.float32)
    partial_value = jnp.concatenate([gate_part, up_part], axis=1)
    slice_width = gate_weight.shape[1]
    summed = lax.psum(partial_value.astype(jnp.bfloat16), "mp").astype(jnp.float32)
    hidden = (jax.nn.silu(summed[:, :slice_width]) * summed[:, slice_width:]).astype(jnp.bfloat16)
    block_rows = hidden
    mlp_float = lax.psum_scatter(
        jnp.dot(block_rows, down_weight, preferred_element_type=jnp.float32).astype(jnp.bfloat16),
        "batch",
        scatter_dimension=0,
        tiled=True,
    )
    return (
        attn_out.reshape(prompts_here, length, model_cols),
        mlp_float.reshape(prompts_here, length, model_cols),
    )


def solution(mesh):
    placed = (
        P("batch", None, "mp"),
        P("batch", None, "mp"),
        P("batch", None, None),
        P("batch", None, None),
        P(),
        P(),
        P("batch", "mp"),
        P("mp"),
        P("mp", "batch"),
        P("mp", "batch"),
        P("batch", "mp"),
    )
    return jax.shard_map(
        body,
        mesh=mesh,
        in_specs=placed,
        out_specs=(P("batch", None, "mp"), P("batch", None, "mp")),
        check_vma=False,
    )
```

profile of v0, /device:TPU:0, one launch (start us, length us, event | category | flops | bytes accessed | tf_op | source)
XLA Modules:
  0.0 413.6 jit_solution(484651136919230348)
XLA Ops:
  7.2 0.0 copy-start
  7.2 0.0 all-gather.9.cloned.1.call-start
  7.3 0.7 compare_select_fusion.1
  7.9 0.7 compare_and_fusion.1
  8.6 0.9 copy.37
  9.6 0.6 gather_fusion.2
  10.2 0.3 fusion.7
  10.4 0.1 fusion.41
  10.5 0.9 bitcast_bitcast_fusion.1
  11.4 0.6 gather_fusion.1
  11.9 0.0 copy-start.6
  12.0 0.0 copy-start.4
  12.0 0.3 fusion.9
  12.3 17.4 %all_gather.12 = bf16[1,64,4096]{2,1,0:T(8,128)(2,1)S(1)} all-gather(bf16[1,64,1024]{2,1,0:T(8,128)(2,1)S(1)} %bitcast.109), channel_id=1, replica_groups=mesh['batch'=8,'mp'=4] {'mp'}, dimensions={2}, use_global_device_ids=true | all-gather | bytes 655360 | tf_op jit(solution)/shard_map/all_gather | solution.py:53
  29.6 0.1 copy.38
  29.7 0.0 copy-start.2
  29.7 0.2 copy.30
  30.0 0.6 gather_fusion
  30.5 0.1 select_bitcast_fusion
  30.6 0.1 copy.31
  30.7 0.8 reshape.200
  31.5 0.0 all-gather.9.cloned.1.call-update
  31.5 0.0 all-gather.5.cloned.1.call-start
  31.6 0.7 all-gather.5.cloned.1.call-update
  32.3 0.0 all-gather.7.cloned.1.call-start
  32.3 0.6 dynamic-slice.2
  33.5 0.1 fusion.30
  33.6 27.7 %all-gather.9.cloned.1.call-done = bf16[8,1,65536]{2,1,0:T(2,128)(2,1)} async-done(((bf16[1,1,65536]{2,1,0:T(2,128)(2,1)}), bf16[8,1,65536]{2,1,0:T(2,128)(2,1)}) %all-gather.9.cloned.1.call-update) | async-done | bytes 1048592 | tf_op jit(solution)/shard_map/all_gather | solution.py:60
  61.3 2.9 fusion.11
  64.2 0.4 fusion.10
  64.6 88.5 %all-gather.5.cloned.1.call-done = bf16[4096,2048]{1,0:T(8,128)(2,1)} async-done(((bf16[512,2048]{1,0:T(8,128)(2,1)}), bf16[4096,2048]{1,0:T(8,128)(2,1)}) %all-gather.5.cloned.1.call-update) | async-done | bytes 16777232 | tf_op jit(solution)/shard_map/all_gather | solution.py:74
  153.1 8.9 %multiply_reduce_fusion = (f32[64]{0:T(128)S(1)}, f32[64,2048]{1,0:T(8,128)S(1)}) fusion(bf16[1,64,2048]{2,1,0:T(8,128)(2,1)S(1)} %copy-done.2, bf16[4096,2048]{1,0:T(8,128)(2,1)} %all-gather.5.cloned.1.call-done, bf16[8,8,32,128]{3,2,1,0:T(8,128)(2,1)S(1)} %bitcast.106), kind=kOutput, calls=%fused_computation.29 | convolution fusion | flops 1074266112 | bytes 18088192 | tf_op jit(solution)/shard_map/dot_general | solution.py:72
  162.0 11.7 %psum.14 = f32[64]{0:T(128)S(1)} all-reduce(f32[64]{0:T(128)S(1)} %get-tuple-element.16), channel_id=1, replica_groups=mesh['batch'=8,'mp'=4] {'mp'}, use_global_device_ids=true, to_apply=%region_4.6 | all-reduce | flops 64 | bytes 512 | tf_op jit(solution)/shard_map/psum | solution.py:79
  173.7 0.8 multiply_convert_fusion
  174.6 0.0 all-gather.7.cloned.1.call-update
  174.6 0.2 all-reduce.2.cloned.1.call-start
  174.8 25.1 %all-gather.7.cloned.1.call-done = bf16[512,2048]{1,0:T(8,128)(2,1)} async-done(((bf16[64,2048]{1,0:T(8,128)(2,1)}), bf16[512,2048]{1,0:T(8,128)(2,1)}) %all-gather.7.cloned.1.call-update) | async-done | bytes 2097168 | tf_op jit(solution)/shard_map/all_gather | solution.py:82
  199.9 7.8 %convolution_convert_fusion.1 = bf16[512,1792]{1,0:T(8,128)(2,1)S(1)} fusion(bf16[512,2048]{1,0:T(8,128)(2,1)} %all-gather.7.cloned.1.call-done, bf16[2048,1792]{1,0:T(8,128)(2,1)} %param.22), kind=kOutput, calls=%fused_computation.8 | convolution fusion | flops 3759013888 | bytes 11272192 | tf_op jit(solution)/shard_map/dot_general | solution.py:84
  207.7 7.0 %convolution_convert_fusion.2 = bf16[512,1792]{1,0:T(8,128)(2,1)S(1)} fusion(bf16[512,2048]{1,0:T(8,128)(2,1)S(1)} %copy-done.5, bf16[2048,1792]{1,0:T(8,128)(2,1)} %param.21), kind=kOutput, calls=%fused_computation.9 | convolution fusion | flops 3759013888 | bytes 11272192 | tf_op jit(solution)/shard_map/dot_general | solution.py:83
  214.7 2.1 pad_maximum_fusion
  216.8 0.0 all-reduce.2.cloned.1.call-update
  216.9 0.0 reduce-scatter.2.cloned.1.call-start
  216.9 138.2 %all-reduce.2.cloned.1.call-done = bf16[512,3584]{1,0:T(8,128)(2,1)} async-done(((bf16[512,3584]{1,0:T(8,128)(2,1)}), bf16[512,3584]{1,0:T(8,128)(2,1)}) %all-reduce.2.cloned.1.call-update) | async-done | bytes 3670032 | tf_op jit(solution)/shard_map/psum | solution.py:87
  355.1 3.0 convert_element_type.62
  358.1 0.0 copy-start.1
  358.1 8.5 %convolution_convert_fusion = bf16[512,2048]{1,0:T(8,128)(2,1)} fusion(bf16[1792,2048]{1,0:T(8,128)(2,1)} %param.23, f32[512,3584]{1,0:T(8,128)S(1)} %convert_element_type.62), kind=kOutput, calls=%fused_computation.7 | convolution fusion | flops 3764649984 | bytes 16777216 | tf_op jit(solution)/shard_map/dot_general | solution.py:91
  366.6 0.0 reduce-scatter.2.cloned.1.call-update
  366.7 40.4 %reduce-scatter.2.cloned.1.call-done = bf16[64,2048]{1,0:T(8,128)(2,1)} async-done(((bf16[512,2048]{1,0:T(8,128)(2,1)}), bf16[64,2048]{1,0:T(8,128)(2,1)}) %reduce-scatter.2.cloned.1.call-update) | async-done | bytes 262160 | tf_op jit(solution)/shard_map/reduce_scatter | solution.py:90
  (17 shorter events, 0.1 us)
Async XLA Ops:
  7.2 1.5 copy-start
  7.2 54.1 %all-gather.9.cloned.1.call-start = ((), (), s32[]{:S(2)}) async-start(), calls=%async_computation.5 | async-start | bytes 2359296 | tf_op jit(solution)/shard_map/all_gather | solution.py:60
  11.9 20.4 %copy-start.6 = (s32[8]{0:T(128)S(1)}, s32[8]{0:T(128)}, u32[]{:S(2)}) copy-start(s32[8]{0:T(128)} %param.17) | copy-start | bytes 100
  12.0 21.6 %copy-start.4 = (s32[8]{0:T(128)S(1)}, s32[8]{0:T(128)}, u32[]{:S(2)}) copy-start(s32[8]{0:T(128)} %param.18) | copy-start | bytes 100
  29.7 123.4 %copy-start.2 = (bf16[1,64,2048]{2,1,0:T(8,128)(2,1)S(1)}, bf16[1,64,2048]{2,1,0:T(8,128)(2,1)}, u32[]{:S(2)}) copy-start(bf16[1,64,2048]{2,1,0:T(8,128)(2,1)} %param.13) | copy-start | bytes 786436
  31.5 121.6 %all-gather.5.cloned.1.call-start = ((), (), s32[]{:S(2)}) async-start(), calls=%async_computation.1 | async-start | bytes 18874368 | tf_op jit(solution)/shard_map/all_gather | solution.py:74
  32.3 167.6 %all-gather.7.cloned.1.call-start = ((), (), s32[]{:S(2)}) async-start(), calls=%async_computation.2 | async-start | bytes 2359296 | tf_op jit(solution)/shard_map/all_gather | solution.py:82
  153.1 20.6 %copy-start.3 = (f32[2048]{0:T(1024)S(1)}, f32[2048]{0:T(1024)}, u32[]{:S(2)}) copy-start(f32[2048]{0:T(1024)} %param.20) | copy-start | bytes 24580
  174.6 180.5 %all-reduce.2.cloned.1.call-start = ((), (), s32[]{:S(2)}) async-start(), calls=%async_computation.3 | async-start | bytes 7340032 | tf_op jit(solution)/shard_map/psum | solution.py:87
  199.9 7.8 %copy-start.5 = (bf16[512,2048]{1,0:T(8,128)(2,1)S(1)}, bf16[512,2048]{1,0:T(8,128)(2,1)}, u32[]{:S(2)}) copy-start(bf16[512,2048]{1,0:T(8,128)(2,1)} %all-gather.7.cloned.1.call-done) | copy-start | bytes 6291460
  216.9 190.2 %reduce-scatter.2.cloned.1.call-start = ((), (), s32[]{:S(2)}) async-start(), calls=%async_computation.4 | async-start | bytes 2359296 | tf_op jit(solution)/shard_map/reduce_scatter | solution.py:90
  358.1 49.0 %copy-start.1 = (bf16[1,64,512]{2,1,0:T(8,128)(2,1)S(1)}, bf16[1,64,512]{2,1,0:T(8,128)(2,1)}, u32[]{:S(2)}) copy-start(bf16[1,64,512]{2,1,0:T(8,128)(2,1)} %param.15) | copy-start | bytes 196612
Sparse Core Ops, SparseCore 0:
  31.6 29.6 all-gather.8
  63.2 89.8 all-gather.4
  174.7 25.1 all-gather.6
  217.0 138.0 all-reduce.1
  366.8 40.2 reduce-scatter.1
where the time goes:
time: 414 us
  waiting for transfers between devices  321 us (78%)
  matrix products  36.1 us (9%)
  blocking collectives  29.1 us (7%)
  between operations  14.6 us (4%)
  other arithmetic  7.56 us (2%)
  local copies, waits for them, and re-layouts  5.31 us (1%)
    psum x1, waiting for transfers between devices, body(): lax.psum(partial_value.astype(jnp.bfloat16), 'mp').astype(jnp.float32)  138 us
    all_gather x1, waiting for transfers between devices, body(): lax.all_gather(out_weight, 'batch', axis=0, tiled=True)  88.5 us
    reduce_scatter x1, waiting for transfers between devices, body(): lax.psum_scatter(jnp.dot(block_rows, down_weight, preferred_element_type=...  40.4 us
    all_gather x1, waiting for transfers between devices, body(): block_rows = lax.all_gather(picked_cols, 'batch', axis=0, tiled=True)  27.7 us
    all_gather x1, waiting for transfers between devices, body(): block_rows = lax.all_gather(normed, 'batch', axis=0, tiled=True)  25.1 us
    all_gather x1, blocking collectives, body(): all_heads = lax.all_gather(head_block, 'mp', axis=2, tiled=True)  17.4 us
    psum x1, blocking collectives, body(): squares = lax.psum(jnp.sum(hidden_state * hidden_state, axis=1), 'mp')  11.7 us
    dot_general x1, matrix products, body(): jnp.dot(mixed_heads, lax.all_gather(out_weight, 'batch', axis=0, tiled=Tr...  8.92 us
  transfers between devices with their start and end apart: 5, of which 5 were waited for; matrix products, arithmetic and copies ran while one was open for 1% of the time, Pallas kernels for 0%

commit v1 on v0

--- a/solution.py
+++ b/solution.py
@@ -9,6 +9,12 @@
 KV = 4
 HD = 128
 ABLATED = 8
+
+
+def gather_and_add(block, axis):
+    parts = lax.all_gather(block, axis, axis=0, tiled=False)
+    total = parts.sum(axis=0)
+    return total
 
 
 def local_heads(query_states, key_states, value_states):
@@ -84,7 +90,7 @@
     up_part = jnp.dot(block_rows, up_weight, preferred_element_type=jnp.float32)
     partial_value = jnp.concatenate([gate_part, up_part], axis=1)
     slice_width = gate_weight.shape[1]
-    summed = lax.psum(partial_value.astype(jnp.bfloat16), "mp").astype(jnp.float32)
+    summed = gather_and_add(partial_value.astype(jnp.bfloat16), "mp").astype(jnp.float32)
     hidden = (jax.nn.silu(summed[:, :slice_width]) * summed[:, slice_width:]).astype(jnp.bfloat16)
     block_rows = hidden
     mlp_float = lax.psum_scatter(

time: 414 us -> 538 us (1.30)
  waiting for transfers between devices: 321 us -> 434 us
  other arithmetic: 7.56 us -> 18.2 us
    all_gather x0 -> x1, waiting for transfers between devices: none -> 253 us  [gather_and_add(): parts = lax.all_gather(block, axis, axis=0, tiled=False)]
    psum x1 -> x0, waiting for transfers between devices: 138 us -> none  [body(): lax.psum(partial_value.astype(jnp.bfloat16), 'mp').astype(jnp.float32)]
    reduce_sum x0 -> x1, other arithmetic: none -> 10.7 us  [gather_and_add(): total = parts.sum(axis=0)]
where the time goes in v1:
time: 538 us
  waiting for transfers between devices  434 us (81%)
  matrix products  36.1 us (7%)
  blocking collectives  29.1 us (5%)
  other arithmetic  18.2 us (3%)
  between operations  14.6 us (3%)
    all_gather x1, waiting for transfers between devices, gather_and_add(): parts = lax.all_gather(block, axis, axis=0, tiled=False)  253 us
    all_gather x1, waiting for transfers between devices, body(): lax.all_gather(out_weight, 'batch', axis=0, tiled=True)  88.5 us
    reduce_scatter x1, waiting for transfers between devices, body(): lax.psum_scatter(jnp.dot(block_rows, down_weight, preferred_element_type=...  39.6 us
    all_gather x1, waiting for transfers between devices, body(): block_rows = lax.all_gather(picked_cols, 'batch', axis=0, tiled=True)  27.7 us
    all_gather x1, waiting for transfers between devices, body(): block_rows = lax.all_gather(normed, 'batch', axis=0, tiled=True)  25.1 us
    all_gather x1, blocking collectives, body(): all_heads = lax.all_gather(head_block, 'mp', axis=2, tiled=True)  17.4 us
    psum x1, blocking collectives, body(): squares = lax.psum(jnp.sum(hidden_state * hidden_state, axis=1), 'mp')  11.7 us
  transfers between devices with their start and end apart: 5, of which 5 were waited for; matrix products, arithmetic and copies ran while one was open for 1% of the time, Pallas kernels for 0%

profile of v1, /device:TPU:0, one launch (start us, length us, event | category | flops | bytes accessed | tf_op | source)
XLA Modules:
  0.0 537.8 jit_solution(1538323809379130294)
XLA Ops:
  7.2 0.0 copy-start
  7.2 0.0 all-gather.12.cloned.1.call-start
  7.3 0.7 compare_select_fusion.1
  7.9 0.7 compare_and_fusion.1
  8.6 0.9 copy.37
  9.6 0.6 gather_fusion.2
  10.2 0.3 fusion.9
  10.4 0.1 fusion.43
  10.5 0.9 bitcast_bitcast_fusion.1
  11.4 0.6 gather_fusion.1
  11.9 0.0 copy-start.6
  12.0 0.0 copy-start.4
  12.0 0.3 fusion.11
  12.3 17.4 %all_gather.16 = bf16[1,64,4096]{2,1,0:T(8,128)(2,1)S(1)} all-gather(bf16[1,64,1024]{2,1,0:T(8,128)(2,1)S(1)} %bitcast.113), channel_id=1, replica_groups=mesh['batch'=8,'mp'=4] {'mp'}, dimensions={2}, use_global_device_ids=true | all-gather | bytes 655360 | tf_op jit(solution)/shard_map/all_gather | solution.py:59
  29.6 0.1 copy.38
  29.7 0.0 copy-start.2
  29.7 0.2 copy.30
  30.0 0.6 gather_fusion
  30.5 0.1 select_bitcast_fusion
  30.6 0.1 copy.31
  30.7 0.8 reshape.231
  31.5 0.0 all-gather.12.cloned.1.call-update
  31.5 0.0 all-gather.6.cloned.1.call-start
  31.6 0.7 all-gather.6.cloned.1.call-update
  32.3 0.0 all-gather.8.cloned.1.call-start
  32.3 0.6 dynamic-slice.2
  33.5 0.1 fusion.32
  33.6 27.7 %all-gather.12.cloned.1.call-done = bf16[8,1,65536]{2,1,0:T(2,128)(2,1)} async-done(((bf16[1,1,65536]{2,1,0:T(2,128)(2,1)}), bf16[8,1,65536]{2,1,0:T(2,128)(2,1)}) %all-gather.12.cloned.1.call-update) | async-done | bytes 1048592 | tf_op jit(solution)/shard_map/all_gather | solution.py:66
  61.3 2.9 fusion.13
  64.2 0.4 fusion.12
  64.6 88.5 %all-gather.6.cloned.1.call-done = bf16[4096,2048]{1,0:T(8,128)(2,1)} async-done(((bf16[512,2048]{1,0:T(8,128)(2,1)}), bf16[4096,2048]{1,0:T(8,128)(2,1)}) %all-gather.6.cloned.1.call-update) | async-done | bytes 16777232 | tf_op jit(solution)/shard_map/all_gather | solution.py:80
  153.1 8.9 %multiply_reduce_fusion = (f32[64]{0:T(128)S(1)}, f32[64,2048]{1,0:T(8,128)S(1)}) fusion(bf16[1,64,2048]{2,1,0:T(8,128)(2,1)S(1)} %copy-done.2, bf16[4096,2048]{1,0:T(8,128)(2,1)} %all-gather.6.cloned.1.call-done, bf16[8,8,32,128]{3,2,1,0:T(8,128)(2,1)S(1)} %bitcast.110), kind=kOutput, calls=%fused_computation.31 | convolution fusion | flops 1074266112 | bytes 18088192 | tf_op jit(solution)/shard_map/dot_general | solution.py:78
  162.0 11.7 %psum.7 = f32[64]{0:T(128)S(1)} all-reduce(f32[64]{0:T(128)S(1)} %get-tuple-element.16), channel_id=1, replica_groups=mesh['batch'=8,'mp'=4] {'mp'}, use_global_device_ids=true, to_apply=%region_4.6 | all-reduce | flops 64 | bytes 512 | tf_op jit(solution)/shard_map/psum | solution.py:85
  173.7 0.8 multiply_convert_fusion
  174.6 0.0 all-gather.8.cloned.1.call-update
  174.6 0.2 all-gather.10.cloned.1.call-start
  174.8 25.1 %all-gather.8.cloned.1.call-done = bf16[512,2048]{1,0:T(8,128)(2,1)} async-done(((bf16[64,2048]{1,0:T(8,128)(2,1)}), bf16[512,2048]{1,0:T(8,128)(2,1)}) %all-gather.8.cloned.1.call-update) | async-done | bytes 2097168 | tf_op jit(solution)/shard_map/all_gather | solution.py:88
  199.9 7.8 %fusion.2 = bf16[1,512,1792]{2,1,0:T(8,128)(2,1)S(1)} fusion(bf16[512,2048]{1,0:T(8,128)(2,1)} %all-gather.8.cloned.1.call-done, bf16[2048,1792]{1,0:T(8,128)(2,1)} %param.21), kind=kOutput, calls=%fused_computation.10 | convolution fusion | flops 3759013888 | bytes 11272192 | tf_op jit(solution)/shard_map/dot_general | solution.py:89
  207.7 7.0 %fusion.3 = bf16[1,512,1792]{2,1,0:T(8,128)(2,1)S(1)} fusion(bf16[512,2048]{1,0:T(8,128)(2,1)S(1)} %copy-done.5, bf16[2048,1792]{1,0:T(8,128)(2,1)} %param.22), kind=kOutput, calls=%fused_computation.11 | convolution fusion | flops 3759013888 | bytes 11272192 | tf_op jit(solution)/shard_map/dot_general | solution.py:90
  214.7 2.1 pad_maximum_fusion
  216.8 0.0 all-gather.10.cloned.1.call-update
  216.8 0.0 reduce-scatter.2.cloned.1.call-start
  216.9 252.6 %all-gather.10.cloned.1.call-done = bf16[4,512,3584]{2,1,0:T(8,128)(2,1)} async-done(((bf16[1,512,3584]{2,1,0:T(8,128)(2,1)}), bf16[4,512,3584]{2,1,0:T(8,128)(2,1)}) %all-gather.10.cloned.1.call-update) | async-done | bytes 14680080 | tf_op jit(solution)/shard_map/all_gather | solution.py:15
  469.5 10.7 %reduce_sum.32 = bf16[512,3584]{1,0:T(8,128)(2,1)} reduce(bf16[4,512,3584]{2,1,0:T(8,128)(2,1)} %all-gather.10.cloned.1.call-done, bf16[]{:T(256)} %constant.87.clone.1), dimensions={0}, to_apply=%region_5.7 | reduce | flops 5505024 | bytes 18350082 | tf_op jit(solution)/shard_map/reduce_sum | solution.py:16
  480.1 3.0 convert_element_type.71
  483.2 8.5 %convolution_convert_fusion = bf16[512,2048]{1,0:T(8,128)(2,1)} fusion(bf16[1792,2048]{1,0:T(8,128)(2,1)} %param.23, f32[512,3584]{1,0:T(8,128)S(1)} %convert_element_type.71), kind=kOutput, calls=%fused_computation.7 | convolution fusion | flops 3764649984 | bytes 16777216 | tf_op jit(solution)/shard_map/dot_general | solution.py:97
  491.7 0.0 reduce-scatter.2.cloned.1.call-update
  491.7 39.6 %reduce-scatter.2.cloned.1.call-done = bf16[64,2048]{1,0:T(8,128)(2,1)} async-done(((bf16[512,2048]{1,0:T(8,128)(2,1)}), bf16[64,2048]{1,0:T(8,128)(2,1)}) %reduce-scatter.2.cloned.1.call-update) | async-done | bytes 262160 | tf_op jit(solution)/shard_map/reduce_scatter | solution.py:96
  (18 shorter events, 0.1 us)
Async XLA Ops:
  7.2 1.5 copy-start
  7.2 54.1 %all-gather.12.cloned.1.call-start = ((), (), s32[]{:S(2)}) async-start(), calls=%async_computation.5 | async-start | bytes 2359296 | tf_op jit(solution)/shard_map/all_gather | solution.py:66
  11.9 20.4 %copy-start.6 = (s32[8]{0:T(128)S(1)}, s32[8]{0:T(128)}, u32[]{:S(2)}) copy-start(s32[8]{0:T(128)} %param.17) | copy-start | bytes 100
  12.0 21.6 %copy-start.4 = (s32[8]{0:T(128)S(1)}, s32[8]{0:T(128)}, u32[]{:S(2)}) copy-start(s32[8]{0:T(128)} %param.18) | copy-start | bytes 100
  29.7 123.4 %copy-start.2 = (bf16[1,64,2048]{2,1,0:T(8,128)(2,1)S(1)}, bf16[1,64,2048]{2,1,0:T(8,128)(2,1)}, u32[]{:S(2)}) copy-start(bf16[1,64,2048]{2,1,0:T(8,128)(2,1)} %param.13) | copy-start | bytes 786436
  31.5 121.6 %all-gather.6.cloned.1.call-start = ((), (), s32[]{:S(2)}) async-start(), calls=%async_computation.1 | async-start | bytes 18874368 | tf_op jit(solution)/shard_map/all_gather | solution.py:80
  32.3 167.6 %all-gather.8.cloned.1.call-start = ((), (), s32[]{:S(2)}) async-start(), calls=%async_computation.2 | async-start | bytes 2359296 | tf_op jit(solution)/shard_map/all_gather | solution.py:88
  153.1 20.6 %copy-start.3 = (f32[2048]{0:T(1024)S(1)}, f32[2048]{0:T(1024)}, u32[]{:S(2)}) copy-start(f32[2048]{0:T(1024)} %param.20) | copy-start | bytes 24580
  174.6 294.9 %all-gather.10.cloned.1.call-start = ((), (), s32[]{:S(2)}) async-start(), calls=%async_computation.3 | async-start | bytes 18350080 | tf_op jit(solution)/shard_map/all_gather | solution.py:15
  199.9 7.8 %copy-start.5 = (bf16[512,2048]{1,0:T(8,128)(2,1)S(1)}, bf16[512,2048]{1,0:T(8,128)(2,1)}, u32[]{:S(2)}) copy-start(bf16[512,2048]{1,0:T(8,128)(2,1)} %all-gather.8.cloned.1.call-done) | copy-start | bytes 6291460
  216.8 314.5 %reduce-scatter.2.cloned.1.call-start = ((), (), s32[]{:S(2)}) async-start(), calls=%async_computation.4 | async-start | bytes 2359296 | tf_op jit(solution)/shard_map/reduce_scatter | solution.py:96
  483.1 48.2 %copy-start.1 = (bf16[1,64,512]{2,1,0:T(8,128)(2,1)S(1)}, bf16[1,64,512]{2,1,0:T(8,128)(2,1)}, u32[]{:S(2)}) copy-start(bf16[1,64,512]{2,1,0:T(8,128)(2,1)} %param.15) | copy-start | bytes 196612
Sparse Core Ops, SparseCore 0:
  31.6 29.6 all-gather.11
  63.2 89.8 all-gather.5
  174.7 25.1 all-gather.7
  217.0 252.4 all-gather.9
  491.8 39.4 reduce-scatter.1
